TPU v7x, 512 devices: a whole 4x4x16 slice. The times are simulated.
512 devices in a mesh: dp: 64 (over z, y_lo, core), tensor: 8 (over x, y_hi).
Axes of the slice: x: 4, y: 4 (y_hi: 2, y_lo: 2; y = y_hi * 2 + y_lo), z: 16, core: 2. Of those that a mesh axis runs over, the one named last changes fastest.
Arguments:
- activations: bfloat16 [98304, 2048], P('dp', 'tensor'), may hold values from -6 to 6
- out_grads: bfloat16 [98304, 2048], P('dp', 'tensor'), may hold values from -0.001953125 to 0.001953125
- left_stat: float32 [2048, 2048], P('dp', 'tensor'), may hold values from -1 to 11, as said below
- right_stat: float32 [2048, 2048], P('dp', 'tensor'), may hold values from -1 to 11, as said below
Outputs:
- left_new: float32 [2048, 2048], P('dp', 'tensor')
- right_new: float32 [2048, 2048], P('dp', 'tensor')
- update: float32 [2048, 2048], P('dp', 'tensor')
Inputs may be any that keep to these rules, and one draw needn't show every extreme that they name: `left_stat`: symmetric, with a positive diagonal. `right_stat`: symmetric, with a positive diagonal.
All inputs are finite; a program needn't handle non-finite values.
Results may differ from a plain program's by a relative error of at most 0.0012.
Values may be sent and summed in bfloat16 or wider, within the bound.
A program may use at most 64 MiB of HBM per device.

v0:
```python
import jax
import jax.numpy as jnp
from jax import lax
from jax.sharding import Mesh
from jax.sharding import PartitionSpec as P

TENSOR = ("tensor_0", "tensor_1")
DP = ("dp_0", "dp_1", "dp_2")
DP_TENSOR = ("dp_0", "dp_1", "dp_2", "tensor_0", "tensor_1")


def in_blocks(x, dim, length):
    lengths = x.shape
    blocks = x.reshape(*lengths[:dim], length, lengths[dim] // length, *lengths[dim + 1 :])
    return jnp.moveaxis(blocks, dim, 0)


def sum_at_owner(x, axis, dim):
    length = lax.axis_size(axis)
    blocks = lax.all_to_all(in_blocks(x, dim, length), axis, 0, 0, tiled=True)
    return jnp.sum(blocks, axis=0)


def in_order(blocks, dim):
    blocks = jnp.moveaxis(blocks, 0, dim)
    lengths = blocks.shape
    return blocks.reshape(*lengths[:dim], lengths[dim] * lengths[dim + 1], *lengths[dim + 2 :])


def gather_in_order(x, axes, turns):
    blocks = x
    for k in turns:
        blocks = lax.all_gather(blocks, axes[k])
    done = turns[::-1]
    back = [done.index(k) for k in range(len(axes))]
    blocks = blocks.transpose(*back, *range(len(axes), blocks.ndim))
    return blocks.reshape(-1, *x.shape)


def gathered_by_axis(x, axes, turns, dim):
    return in_order(gather_in_order(x, axes, turns), dim)


def side_by_side(arrays, axis, dim, along):
    both = jnp.concatenate(arrays, axis=along)
    result, at, gathered = (sum_at_owner(both, axis, dim), 0, [])
    for a in arrays:
        gathered.append(lax.slice_in_dim(result, at, at + a.shape[along], axis=along))
        at += a.shape[along]
    return tuple(gathered)


def by_axis(x, axes):
    for axis in axes:
        x = lax.psum(x, axis)
    return x


def sent_to_all(x, axis):
    length = lax.axis_size(axis)
    return lax.all_to_all(jnp.broadcast_to(x[None], (length, *x.shape)), axis, 0, 0, tiled=True)


def gather_directly(x, axis, dim):
    return in_order(sent_to_all(x, axis), dim)


def local(activations, out_grads, left_stat, right_stat):
    highest = lax.Precision.HIGHEST
    tensor_count = lax.axis_size(TENSOR)
    dp_count = lax.axis_size(DP)
    col_count = out_grads.shape[1]
    full_order = col_count * tensor_count
    row_count = full_order // dp_count
    grad_terms = lax.dot_general(
        lax.all_gather(activations, TENSOR, axis=1, tiled=True),
        out_grads,
        (((0,), (0,)), ((), ())),
        preferred_element_type=jnp.float32,
    )
    grad_block = sum_at_owner(grad_terms, DP, 0)
    grad_cols = gathered_by_axis(grad_block, DP, (1, 0, 2), 0)
    left_part = lax.dot_general(
        grad_block,
        grad_cols,
        (((1,), (1,)), ((), ())),
        precision=highest,
        preferred_element_type=jnp.float32,
    )
    dp_place = lax.axis_index(DP)
    row_start = dp_place * row_count
    tensor_rows = lax.all_to_all(grad_cols, TENSOR, split_axis=0, concat_axis=1, tiled=True)
    strip_cols = lax.dynamic_slice_in_dim(tensor_rows, row_start, row_count, 1)
    right_part = lax.dot_general(
        strip_cols,
        tensor_rows,
        (((0,), (0,)), ((), ())),
        precision=highest,
        preferred_element_type=jnp.float32,
    )
    left_sum, right_sum = side_by_side((left_part, right_part), TENSOR, 1, 0)
    left_new = 0.9 * left_stat + 0.1 * left_sum
    right_new = 0.9 * right_stat + 0.1 * right_sum
    left_sq = jnp.sum(left_new * left_new)
    right_sq = jnp.sum(right_new * right_new)
    grad_sq = jnp.sum(grad_block * grad_block)
    left_total, right_total, grad_total = (
        by_axis(left_sq, DP_TENSOR),
        by_axis(right_sq, DP_TENSOR),
        by_axis(grad_sq, DP_TENSOR),
    )
    left_scale = jnp.sqrt(left_total / full_order + 1e-06)
    right_scale = jnp.sqrt(right_total / full_order + 1e-06)
    left_whole = gather_directly(left_new, TENSOR, 1)
    left_product = jnp.dot(
        left_whole, grad_cols, precision=highest, preferred_element_type=jnp.float32
    )
    pre_left = 5.0 * grad_block - left_product / left_scale
    pre_rows = gather_directly(pre_left, TENSOR, 1)
    right_product = jnp.dot(
        pre_rows,
        lax.all_gather(right_new.astype(jnp.bfloat16), DP, axis=0, tiled=True).astype(jnp.float32),
        precision=highest,
        preferred_element_type=jnp.float32,
    )
    pre_block = 5.0 * pre_left - right_product / right_scale
    pre_sq = jnp.sum(pre_block * pre_block)
    pre_total = by_axis(pre_sq, DP_TENSOR)
    factor = jnp.sqrt(grad_total + 1e-06) / jnp.sqrt(pre_total + 1e-06)
    return (left_new, right_new, pre_block * factor)


def solution(mesh):
    finer = Mesh(
        mesh.devices.reshape(16, 2, 2, 4, 2), ("dp_0", "dp_1", "dp_2", "tensor_0", "tensor_1")
    )
    placed = (P(DP, TENSOR), P(DP, TENSOR), P(DP, TENSOR), P(DP, TENSOR))
    return jax.shard_map(
        local,
        mesh=finer,
        in_specs=placed,
        out_specs=(P(DP, TENSOR), P(DP, TENSOR), P(DP, TENSOR)),
        check_vma=False,
    )
```

profile of v0, /device:TPU:16, one launch (start us, length us, event | category | flops | bytes accessed | tf_op | source)
XLA Modules:
  0.0 582.7 jit_solution(15723450914595324753)
XLA Ops:
  7.2 0.0 copy-start
  7.2 0.0 all-gather.8.cloned.1.call-start
  7.2 0.7 all-gather.8.cloned.1.call-update
  7.9 0.0 all-gather.12.cloned.1.call-start
  8.0 119.7 %all-gather.8.cloned.1.call-done = bf16[1536,2048]{1,0:T(8,128)(2,1)} async-done(((bf16[1536,256]{1,0:T(8,128)(2,1)}), bf16[1536,2048]{1,0:T(8,128)(2,1)}) %all-gather.8.cloned.1.call-update) | async-done | bytes 6291472 | tf_op jit(solution)/shard_map/all_gather | solution.py:76
  127.6 0.0 copy-done
  127.6 4.7 fusion.10
  132.4 115.6 %all_to_all.39 = f32[64,32,256]{2,1,0:T(8,128)S(1)} all-to-all(f32[64,32,256]{2,1,0:T(8,128)S(1)} %bitcast.35), channel_id=1, replica_groups=mesh['dp_0'=16,'dp_1'=2,'dp_2'=2,'tensor_0'=4,'tensor_1'=2] {'dp_0','dp_..., dimensions={0} | all-to-all | bytes 4194304 | tf_op jit(solution)/shard_map/all_to_all | solution.py:20
  248.0 0.1 reduce_sum.54
  248.1 4.7 all-gather
  252.8 0.0 all-gather.12.cloned.1.call-update
  252.8 0.0 all-gather.14.cloned.1.call-start
  252.9 61.7 %all-gather.12.cloned.1.call-done = f32[32,32,256]{2,1,0:T(8,128)} async-done(((f32[2,32,256]{2,1,0:T(8,128)}), f32[32,32,256]{2,1,0:T(8,128)}) %all-gather.12.cloned.1.call-update) | async-done | bytes 1048592 | tf_op jit(solution)/shard_map/all_gather | solution.py:33
  314.6 0.0 all-gather.14.cloned.1.call-update
  314.6 20.0 %all-gather.14.cloned.1.call-done = f32[32,2,32,256]{3,2,1,0:T(8,128)} async-done(((f32[16,2,32,256]{3,2,1,0:T(8,128)}), f32[32,2,32,256]{3,2,1,0:T(8,128)}) %all-gather.14.cloned.1.call-update) | async-done | bytes 2097168 | tf_op jit(solution)/shard_map/all_gather | solution.py:33
  334.6 3.2 copy.11
  337.8 7.2 %all-to-all-start.1 = ((f32[8,256,256]{2,1,0:T(8,128)}), f32[8,256,256]{2,1,0:T(8,128)S(1)}, u32[]{:S(2)}, u32[]{:S(2)}) async-start(f32[8,256,256]{2,1,0:T(8,128)} %bitcast.7), calls=%async_computation.1 | async-start | bytes 4194304 | tf_op jit(solution)/shard_map/all_to_all | solution.py:92
  345.0 0.0 all-gather.10.cloned.1.call-start
  345.0 3.6 fusion.11
  348.7 27.0 %all-to-all-done.1 = f32[8,256,256]{2,1,0:T(8,128)S(1)} async-done(((f32[8,256,256]{2,1,0:T(8,128)}), f32[8,256,256]{2,1,0:T(8,128)S(1)}, u32[]{:S(2)}, u32[]{:S(2)}) %all-to-all-start.1) | async-done | bytes 2097184 | tf_op jit(solution)/shard_map/all_to_all | solution.py:92
  375.6 0.0 copy-start.1
  375.6 1.3 copy-done.1
  376.9 1.9 copy.13
  378.9 2.0 fusion.4
  380.9 0.0 copy-start.4
  380.9 0.0 copy-start.5
  381.0 13.0 %all_to_all.40 = f32[8,64,256]{2,1,0:T(8,128)S(1)} all-to-all(f32[8,64,256]{2,1,0:T(8,128)S(1)} %bitcast.37), channel_id=1, replica_groups=mesh['dp_0'=16,'dp_1'=2,'dp_2'=2,'tensor_0'=4,'tensor_1'=2] {'tensor_0',..., dimensions={0} | all-to-all | bytes 1048576 | tf_op jit(solution)/shard_map/all_to_all | solution.py:20
  394.0 0.0 copy-done.4
  394.0 0.0 copy-done.5
  394.0 1.2 fusion.7
  395.2 0.0 copy-start.2
  395.2 0.0 copy-start.3
  395.2 0.0 all-gather.10.cloned.1.call-update
  395.3 0.7 broadcast_in_dim.4
  396.0 5.6 all-to-all-start.3
  401.6 0.7 multiply_reduce_fusion.2
  402.3 32.0 %all-reduce.1 = (f32[]{:T(128)}, f32[]{:T(128)}) all-reduce(f32[]{:T(128)} %get-tuple-element.27, f32[]{:T(128)} %multiply_reduce_fusion.2), channel_id=1, replica_groups=mesh['dp_0'=16,'dp_1'=2,'dp_2'=2,'tensor_0'=4,'tensor_1'=2] {'dp_0'}, use_global_device_ids=true, to_apply=%region_3.0 | all-reduce | flops 2 | bytes 16 | tf_op jit(solution)/shard_map/psum | solution.py:55
  434.3 5.6 all-reduce.9
  439.9 3.2 all-reduce.7
  443.1 11.1 %all-reduce.3 = (f32[]{:T(128)}, f32[]{:T(128)}) all-reduce(f32[]{:T(128)} %get-tuple-element.17, f32[]{:T(128)} %get-tuple-element.18), channel_id=1, replica_groups=mesh['dp_0'=16,'dp_1'=2,'dp_2'=2,'tensor_0'=4,'tensor_1'=2] {'tensor_0'}, use_global_device_ids=true, to_apply=%region_6.0 | all-reduce | flops 2 | bytes 16 | tf_op jit(solution)/shard_map/psum | solution.py:55
  454.2 7.1 %all-reduce.5 = (f32[]{:T(128)}, f32[]{:T(128)}) all-reduce(f32[]{:T(128)} %get-tuple-element.9, f32[]{:T(128)} %get-tuple-element.10), channel_id=1, replica_groups=mesh['dp_0'=16,'dp_1'=2,'dp_2'=2,'tensor_0'=4,'tensor_1'=2] {'tensor_1'}, use_global_device_ids=true, to_apply=%region_7.0 | all-reduce | flops 2 | bytes 16 | tf_op jit(solution)/shard_map/psum | solution.py:55
  462.1 0.0 all-to-all-done.3
  462.1 2.7 fusion.1
  464.8 0.7 broadcast_in_dim.5
  465.5 0.0 copy-done.2
  465.5 0.0 copy-done.3
  465.5 5.1 all-to-all-start.4
  470.6 0.6 multiply_reduce_fusion.1
  471.8 4.9 all-to-all-done.4
  476.8 38.5 %all-gather.10.cloned.1.call-done = bf16[2048,256]{1,0:T(8,128)(2,1)} async-done(((bf16[32,256]{1,0:T(8,128)(2,1)}), bf16[2048,256]{1,0:T(8,128)(2,1)}) %all-gather.10.cloned.1.call-update) | async-done | bytes 1048592 | tf_op jit(solution)/shard_map/all_gather | solution.py:122
  515.3 2.4 multiply_reduce_fusion
  517.7 29.6 %all-reduce = (f32[]{:T(128)}, f32[]{:T(128)}) all-reduce(f32[]{:T(128)} %multiply_reduce_fusion.1, f32[]{:T(128)} %get-tuple-element.29), channel_id=1, replica_groups=mesh['dp_0'=16,'dp_1'=2,'dp_2'=2,'tensor_0'=4,'tensor_1'=2] {'dp_0'}, use_global_device_ids=true, to_apply=%region_15.0 | all-reduce | flops 2 | bytes 16 | tf_op jit(solution)/shard_map/psum | solution.py:55
  547.4 5.6 all-reduce.8
  553.0 3.1 all-reduce.6
  556.1 11.2 %all-reduce.2 = (f32[]{:T(128)}, f32[]{:T(128)}) all-reduce(f32[]{:T(128)} %get-tuple-element.15, f32[]{:T(128)} %get-tuple-element.16), channel_id=1, replica_groups=mesh['dp_0'=16,'dp_1'=2,'dp_2'=2,'tensor_0'=4,'tensor_1'=2] {'tensor_0'}, use_global_device_ids=true, to_apply=%region_18.0 | all-reduce | flops 2 | bytes 16 | tf_op jit(solution)/shard_map/psum | solution.py:55
  567.2 7.1 %all-reduce.4 = (f32[]{:T(128)}, f32[]{:T(128)}) all-reduce(f32[]{:T(128)} %get-tuple-element.7, f32[]{:T(128)} %get-tuple-element.8), channel_id=1, replica_groups=mesh['dp_0'=16,'dp_1'=2,'dp_2'=2,'tensor_0'=4,'tensor_1'=2] {'tensor_1'}, use_global_device_ids=true, to_apply=%region_19.0 | all-reduce | flops 2 | bytes 16 | tf_op jit(solution)/shard_map/psum | solution.py:55
  575.6 0.6 broadcast_multiply_fusion
  (5 shorter events, 0.1 us)
Async XLA Ops:
  7.2 120.5 %copy-start = (bf16[1536,256]{1,0:T(8,128)(2,1)S(1)}, bf16[1536,256]{1,0:T(8,128)(2,1)}, u32[]{:S(2)}) copy-start(bf16[1536,256]{1,0:T(8,128)(2,1)} %param.5) | copy-start | bytes 2359300
  7.2 120.4 %all-gather.8.cloned.1.call-start = ((), (), s32[]{:S(2)}) async-start(), calls=%async_computation.5 | async-start | bytes 7077888 | tf_op jit(solution)/shard_map/all_gather | solution.py:76
  7.9 306.7 %all-gather.12.cloned.1.call-start = ((), (), s32[]{:S(2)}) async-start(), calls=%async_computation.7 | async-start | bytes 1114112 | tf_op jit(solution)/shard_map/all_gather | solution.py:33
  252.8 81.8 %all-gather.14.cloned.1.call-start = ((), (), s32[]{:S(2)}) async-start(), calls=%async_computation.8 | async-start | bytes 3145728 | tf_op jit(solution)/shard_map/all_gather | solution.py:33
  337.8 37.8 %all-to-all-start.1 = ((f32[8,256,256]{2,1,0:T(8,128)}), f32[8,256,256]{2,1,0:T(8,128)S(1)}, u32[]{:S(2)}, u32[]{:S(2)}) async-start(f32[8,256,256]{2,1,0:T(8,128)} %bitcast.7), calls=%async_computation.1 | async-start | bytes 4194304 | tf_op jit(solution)/shard_map/all_to_all | solution.py:92
  345.0 170.2 %all-gather.10.cloned.1.call-start = ((), (), s32[]{:S(2)}) async-start(), calls=%async_computation.6 | async-start | bytes 1064960 | tf_op jit(solution)/shard_map/all_gather | solution.py:122
  375.6 1.3 copy-start.1
  380.9 13.1 %copy-start.4 = (f32[32,256]{1,0:T(8,128)S(1)}, f32[32,256]{1,0:T(8,128)}, u32[]{:S(2)}) copy-start(f32[32,256]{1,0:T(8,128)} %param.7) | copy-start | bytes 98308
  380.9 13.1 %copy-start.5 = (f32[32,256]{1,0:T(8,128)S(1)}, f32[32,256]{1,0:T(8,128)}, u32[]{:S(2)}) copy-start(f32[32,256]{1,0:T(8,128)} %param.6) | copy-start | bytes 98308
  395.2 70.3 %copy-start.2 = (f32[32,256]{1,0:T(8,128)}, f32[32,256]{1,0:T(8,128)S(1)}, u32[]{:S(2)}) copy-start(f32[32,256]{1,0:T(8,128)S(1)} %get-tuple-element.28) | copy-start | bytes 98308
  395.2 70.3 %copy-start.3 = (f32[32,256]{1,0:T(8,128)}, f32[32,256]{1,0:T(8,128)S(1)}, u32[]{:S(2)}) copy-start(f32[32,256]{1,0:T(8,128)S(1)} %get-tuple-element.24) | copy-start | bytes 98308
  396.0 66.1 %all-to-all-start.3 = ((f32[8,32,256]{2,1,0:T(8,128)}), f32[8,32,256]{2,1,0:T(8,128)S(1)}, u32[]{:S(2)}, u32[]{:S(2)}) async-start(f32[8,32,256]{2,1,0:T(8,128)} %broadcast_in_dim.4), calls=%async_computation.3 | async-start | bytes 524288 | tf_op jit(solution)/shard_map/all_to_all | solution.py:61
  465.5 11.2 %all-to-all-start.4 = ((f32[8,32,256]{2,1,0:T(8,128)}), f32[8,32,256]{2,1,0:T(8,128)S(1)}, u32[]{:S(2)}, u32[]{:S(2)}) async-start(f32[8,32,256]{2,1,0:T(8,128)} %broadcast_in_dim.5), calls=%async_computation.4 | async-start | bytes 524288 | tf_op jit(solution)/shard_map/all_to_all | solution.py:61
Sparse Core Ops, SparseCore 0:
  11.1 116.5 all-gather.7
  253.0 61.5 all-gather.11
  316.7 17.9 all-gather.13
  395.4 119.8 all-gather.9
where the time goes:
time: 584 us; the launch traced here: 583 us
  waiting for transfers between devices  273 us (47%)
  blocking collectives  249 us (43%)
  starting transfers between devices  18.1 us (3%)
  between operations  16.5 us (3%)
  matrix products  15.5 us (3%)
  local copies, waits for them, and re-layouts  7.96 us (1%)
    all_to_all x2, blocking collectives, sum_at_owner(): blocks = lax.all_to_all(in_blocks(x, dim, length), axis, 0, 0, tiled=True)  129 us
    all_gather x1, waiting for transfers between devices, local(): lax.all_gather(activations, TENSOR, axis=1, tiled=True)  120 us
    psum x10, blocking collectives, by_axis(): x = lax.psum(x, axis)  116 us
    all_gather x2, waiting for transfers between devices, gather_in_order(): blocks = lax.all_gather(blocks, axes[k])  81.7 us
    all_gather x1, waiting for transfers between devices, local(): lax.all_gather(right_new.astype(jnp.bfloat16), DP, axis=0, tiled=True)  38.5 us
    all_to_all x1, waiting for transfers between devices, local(): lax.all_to_all(grad_cols, TENSOR, split_axis=0, concat_axis=1, tiled=True)  27 us
  transfers between devices with their start and end apart: 7, of which 6 were waited for; matrix products, arithmetic and copies ran while one was open for 2% of the time, Pallas kernels for 0%

commit v1 on v0

--- a/solution.py
+++ b/solution.py
@@ -89,7 +89,10 @@
     )
     dp_place = lax.axis_index(DP)
     row_start = dp_place * row_count
-    tensor_rows = lax.all_to_all(grad_cols, TENSOR, split_axis=0, concat_axis=1, tiled=True)
+    size = lax.axis_size(TENSOR)
+    pieces = jnp.stack(jnp.split(grad_cols, size, axis=0), axis=0)
+    pieces = lax.all_to_all(pieces, TENSOR, split_axis=0, concat_axis=0)
+    tensor_rows = jnp.concatenate(pieces, axis=1)
     strip_cols = lax.dynamic_slice_in_dim(tensor_rows, row_start, row_count, 1)
     right_part = lax.dot_general(
         strip_cols,

time: 584 us -> 590 us (1.010)
  the two profiles are of different devices: /device:TPU:16 before, /device:TPU:8 now
where the time goes in v1:
time: 590 us; the launch traced here: 589 us
  waiting for transfers between devices  277 us (47%)
  blocking collectives  250 us (42%)
  between operations  16.6 us (3%)
  local copies, waits for them, and re-layouts  13.9 us (2%)
  starting transfers between devices  13.9 us (2%)
  matrix products  13.9 us (2%)
    all_to_all x2, blocking collectives, sum_at_owner(): blocks = lax.all_to_all(in_blocks(x, dim, length), axis, 0, 0, tiled=True)  129 us
    all_gather x1, waiting for transfers between devices, local(): lax.all_gather(activations, TENSOR, axis=1, tiled=True)  121 us
    psum x10, blocking collectives, by_axis(): x = lax.psum(x, axis)  116 us
    all_gather x2, waiting for transfers between devices, gather_in_order(): blocks = lax.all_gather(blocks, axes[k])  80.7 us
    all_gather x1, waiting for transfers between devices, local(): lax.all_gather(right_new.astype(jnp.bfloat16), DP, axis=0, tiled=True)  39.3 us
    all_to_all x1, waiting for transfers between devices, local(): pieces = lax.all_to_all(pieces, TENSOR, split_axis=0, concat_axis=0)  28.2 us
  transfers between devices with their start and end apart: 7, of which 6 were waited for; matrix products, arithmetic and copies ran while one was open for 1% of the time, Pallas kernels for 0%

profile of v1, /device:TPU:8, one launch (start us, length us, event | category | flops | bytes accessed | tf_op | source)
XLA Modules:
  0.0 589.4 jit_solution(15135091162974240539)
XLA Ops:
  7.2 0.0 copy-start
  7.2 0.0 all-gather.8.cloned.1.call-start
  7.2 0.7 all-gather.8.cloned.1.call-update
  7.9 0.0 all-gather.12.cloned.1.call-start
  8.0 121.3 %all-gather.8.cloned.1.call-done = bf16[1536,2048]{1,0:T(8,128)(2,1)} async-done(((bf16[1536,256]{1,0:T(8,128)(2,1)}), bf16[1536,2048]{1,0:T(8,128)(2,1)}) %all-gather.8.cloned.1.call-update) | async-done | bytes 6291472 | tf_op jit(solution)/shard_map/all_gather | solution.py:76
  129.3 0.0 copy-done
  129.3 4.7 fusion.11
  134.1 115.0 %all_to_all.25 = f32[64,32,256]{2,1,0:T(8,128)S(1)} all-to-all(f32[64,32,256]{2,1,0:T(8,128)S(1)} %bitcast.44), channel_id=1, replica_groups=mesh['dp_0'=16,'dp_1'=2,'dp_2'=2,'tensor_0'=4,'tensor_1'=2] {'dp_0','dp_..., dimensions={0} | all-to-all | bytes 4194304 | tf_op jit(solution)/shard_map/all_to_all | solution.py:20
  249.1 0.1 reduce_sum.54
  249.2 4.7 all-gather
  253.9 0.0 all-gather.12.cloned.1.call-update
  253.9 0.0 all-gather.14.cloned.1.call-start
  254.0 60.7 %all-gather.12.cloned.1.call-done = f32[32,32,256]{2,1,0:T(8,128)} async-done(((f32[2,32,256]{2,1,0:T(8,128)}), f32[32,32,256]{2,1,0:T(8,128)}) %all-gather.12.cloned.1.call-update) | async-done | bytes 1048592 | tf_op jit(solution)/shard_map/all_gather | solution.py:33
  314.7 0.0 all-gather.14.cloned.1.call-update
  314.7 20.0 %all-gather.14.cloned.1.call-done = f32[32,2,32,256]{3,2,1,0:T(8,128)} async-done(((f32[16,2,32,256]{3,2,1,0:T(8,128)}), f32[32,2,32,256]{3,2,1,0:T(8,128)}) %all-gather.14.cloned.1.call-update) | async-done | bytes 2097168 | tf_op jit(solution)/shard_map/all_gather | solution.py:33
  334.7 1.6 fusion.10
  336.4 0.7 constant_dynamic-update-slice_fusion.7
  337.3 0.7 constant_dynamic-update-slice_fusion.6
  338.0 0.7 constant_dynamic-update-slice_fusion.5
  338.7 0.7 constant_dynamic-update-slice_fusion.4
  339.5 0.7 constant_dynamic-update-slice_fusion.3
  340.2 0.7 constant_dynamic-update-slice_fusion.2
  340.9 0.7 constant_dynamic-update-slice_fusion.1
  341.7 0.7 constant_dynamic-update-slice_fusion
  342.4 5.8 all-to-all-start.1
  348.2 0.0 all-gather.10.cloned.1.call-start
  348.3 1.7 copy.18
  350.0 2.0 fusion.12
  352.0 28.2 %all-to-all-done.1 = f32[8,256,256]{2,1,0:T(8,128)} async-done(((f32[8,256,256]{2,1,0:T(8,128)}), f32[8,256,256]{2,1,0:T(8,128)}, u32[]{:S(2)}, u32[]{:S(2)}) %all-to-all-start.1) | async-done | bytes 2097184 | tf_op jit(solution)/shard_map/all_to_all | solution.py:94
  380.2 2.9 copy.27
  383.1 3.6 fusion.4
  386.8 0.0 copy-start.3
  386.9 14.0 %all_to_all.26 = f32[8,64,256]{2,1,0:T(8,128)S(1)} all-to-all(f32[8,64,256]{2,1,0:T(8,128)S(1)} %bitcast.46), channel_id=1, replica_groups=mesh['dp_0'=16,'dp_1'=2,'dp_2'=2,'tensor_0'=4,'tensor_1'=2] {'tensor_0',..., dimensions={0} | all-to-all | bytes 1048576 | tf_op jit(solution)/shard_map/all_to_all | solution.py:20
  400.9 0.0 copy-done.3
  400.9 2.0 fusion.7
  402.9 0.0 copy-start.1
  402.9 0.0 copy-start.2
  402.9 0.0 all-gather.10.cloned.1.call-update
  403.0 0.7 broadcast_in_dim.4
  403.7 3.4 all-to-all-start.3
  407.1 0.6 multiply_reduce_fusion.2
  407.7 31.9 %all-reduce.1 = (f32[]{:T(128)}, f32[]{:T(128)}) all-reduce(f32[]{:T(128)} %get-tuple-element.35, f32[]{:T(128)} %multiply_reduce_fusion.2), channel_id=1, replica_groups=mesh['dp_0'=16,'dp_1'=2,'dp_2'=2,'tensor_0'=4,'tensor_1'=2] {'dp_0'}, use_global_device_ids=true, to_apply=%region_3.0 | all-reduce | flops 2 | bytes 16 | tf_op jit(solution)/shard_map/psum | solution.py:55
  439.7 5.6 all-reduce.9
  445.3 3.1 all-reduce.7
  448.4 11.6 %all-reduce.3 = (f32[]{:T(128)}, f32[]{:T(128)}) all-reduce(f32[]{:T(128)} %get-tuple-element.17, f32[]{:T(128)} %get-tuple-element.18), channel_id=1, replica_groups=mesh['dp_0'=16,'dp_1'=2,'dp_2'=2,'tensor_0'=4,'tensor_1'=2] {'tensor_0'}, use_global_device_ids=true, to_apply=%region_6.0 | all-reduce | flops 2 | bytes 16 | tf_op jit(solution)/shard_map/psum | solution.py:55
  459.9 7.1 %all-reduce.5 = (f32[]{:T(128)}, f32[]{:T(128)}) all-reduce(f32[]{:T(128)} %get-tuple-element.9, f32[]{:T(128)} %get-tuple-element.10), channel_id=1, replica_groups=mesh['dp_0'=16,'dp_1'=2,'dp_2'=2,'tensor_0'=4,'tensor_1'=2] {'tensor_1'}, use_global_device_ids=true, to_apply=%region_7.0 | all-reduce | flops 2 | bytes 16 | tf_op jit(solution)/shard_map/psum | solution.py:55
  467.7 0.0 all-to-all-done.3
  467.7 1.1 fusion.1
  468.8 0.7 broadcast_in_dim.5
  469.6 0.0 copy-done.1
  469.6 0.0 copy-done.2
  469.6 4.6 all-to-all-start.4
  474.2 0.6 multiply_reduce_fusion.1
  475.5 7.2 %all-to-all-done.4 = f32[8,32,256]{2,1,0:T(8,128)S(1)} async-done(((f32[8,32,256]{2,1,0:T(8,128)}), f32[8,32,256]{2,1,0:T(8,128)S(1)}, u32[]{:S(2)}, u32[]{:S(2)}) %all-to-all-start.4) | async-done | bytes 262176 | tf_op jit(solution)/shard_map/all_to_all | solution.py:61
  482.6 39.3 %all-gather.10.cloned.1.call-done = bf16[2048,256]{1,0:T(8,128)(2,1)} async-done(((bf16[32,256]{1,0:T(8,128)(2,1)}), bf16[2048,256]{1,0:T(8,128)(2,1)}) %all-gather.10.cloned.1.call-update) | async-done | bytes 1048592 | tf_op jit(solution)/shard_map/all_gather | solution.py:125
  522.0 2.4 multiply_reduce_fusion
  524.4 29.7 %all-reduce = (f32[]{:T(128)}, f32[]{:T(128)}) all-reduce(f32[]{:T(128)} %multiply_reduce_fusion.1, f32[]{:T(128)} %get-tuple-element.37), channel_id=1, replica_groups=mesh['dp_0'=16,'dp_1'=2,'dp_2'=2,'tensor_0'=4,'tensor_1'=2] {'dp_0'}, use_global_device_ids=true, to_apply=%region_15.0 | all-reduce | flops 2 | bytes 16 | tf_op jit(solution)/shard_map/psum | solution.py:55
  554.1 5.6 all-reduce.8
  559.8 3.1 all-reduce.6
  562.9 11.1 %all-reduce.2 = (f32[]{:T(128)}, f32[]{:T(128)}) all-reduce(f32[]{:T(128)} %get-tuple-element.15, f32[]{:T(128)} %get-tuple-element.16), channel_id=1, replica_groups=mesh['dp_0'=16,'dp_1'=2,'dp_2'=2,'tensor_0'=4,'tensor_1'=2] {'tensor_0'}, use_global_device_ids=true, to_apply=%region_18.0 | all-reduce | flops 2 | bytes 16 | tf_op jit(solution)/shard_map/psum | solution.py:55
  573.9 7.1 %all-reduce.4 = (f32[]{:T(128)}, f32[]{:T(128)}) all-reduce(f32[]{:T(128)} %get-tuple-element.7, f32[]{:T(128)} %get-tuple-element.8), channel_id=1, replica_groups=mesh['dp_0'=16,'dp_1'=2,'dp_2'=2,'tensor_0'=4,'tensor_1'=2] {'tensor_1'}, use_global_device_ids=true, to_apply=%region_19.0 | all-reduce | flops 2 | bytes 16 | tf_op jit(solution)/shard_map/psum | solution.py:55
  582.3 0.6 broadcast_multiply_fusion
  (13 shorter events, 0.3 us)
Async XLA Ops:
  7.2 122.1 %copy-start = (bf16[1536,256]{1,0:T(8,128)(2,1)S(1)}, bf16[1536,256]{1,0:T(8,128)(2,1)}, u32[]{:S(2)}) copy-start(bf16[1536,256]{1,0:T(8,128)(2,1)} %param.5) | copy-start | bytes 2359300
  7.2 122.1 %all-gather.8.cloned.1.call-start = ((), (), s32[]{:S(2)}) async-start(), calls=%async_computation.5 | async-start | bytes 7077888 | tf_op jit(solution)/shard_map/all_gather | solution.py:76
  7.9 306.8 %all-gather.12.cloned.1.call-start = ((), (), s32[]{:S(2)}) async-start(), calls=%async_computation.7 | async-start | bytes 1114112 | tf_op jit(solution)/shard_map/all_gather | solution.py:33
  253.9 80.8 %all-gather.14.cloned.1.call-start = ((), (), s32[]{:S(2)}) async-start(), calls=%async_computation.8 | async-start | bytes 3145728 | tf_op jit(solution)/shard_map/all_gather | solution.py:33
  342.4 37.8 %all-to-all-start.1 = ((f32[8,256,256]{2,1,0:T(8,128)}), f32[8,256,256]{2,1,0:T(8,128)}, u32[]{:S(2)}, u32[]{:S(2)}) async-start(f32[8,256,256]{2,1,0:T(8,128)} %constant_dynamic-update-slice_fusion), calls=%async_computation.1 | async-start | bytes 4194304 | tf_op jit(solution)/shard_map/all_to_all | solution.py:94
  348.2 173.8 %all-gather.10.cloned.1.call-start = ((), (), s32[]{:S(2)}) async-start(), calls=%async_computation.6 | async-start | bytes 1064960 | tf_op jit(solution)/shard_map/all_gather | solution.py:125
  386.8 14.1 %copy-start.3 = (f32[32,256]{1,0:T(8,128)S(1)}, f32[32,256]{1,0:T(8,128)}, u32[]{:S(2)}) copy-start(f32[32,256]{1,0:T(8,128)} %param.7) | copy-start | bytes 98308
  402.9 66.6 %copy-start.1 = (f32[32,256]{1,0:T(8,128)}, f32[32,256]{1,0:T(8,128)S(1)}, u32[]{:S(2)}) copy-start(f32[32,256]{1,0:T(8,128)S(1)} %get-tuple-element.36) | copy-start | bytes 98308
  402.9 66.6 %copy-start.2 = (f32[32,256]{1,0:T(8,128)}, f32[32,256]{1,0:T(8,128)S(1)}, u32[]{:S(2)}) copy-start(f32[32,256]{1,0:T(8,128)S(1)} %get-tuple-element.24) | copy-start | bytes 98308
  403.7 64.0 %all-to-all-start.3 = ((f32[8,32,256]{2,1,0:T(8,128)}), f32[8,32,256]{2,1,0:T(8,128)S(1)}, u32[]{:S(2)}, u32[]{:S(2)}) async-start(f32[8,32,256]{2,1,0:T(8,128)} %broadcast_in_dim.4), calls=%async_computation.3 | async-start | bytes 524288 | tf_op jit(solution)/shard_map/all_to_all | solution.py:61
  469.6 13.0 %all-to-all-start.4 = ((f32[8,32,256]{2,1,0:T(8,128)}), f32[8,32,256]{2,1,0:T(8,128)S(1)}, u32[]{:S(2)}, u32[]{:S(2)}) async-start(f32[8,32,256]{2,1,0:T(8,128)} %broadcast_in_dim.5), calls=%async_computation.4 | async-start | bytes 524288 | tf_op jit(solution)/shard_map/all_to_all | solution.py:61
Sparse Core Ops, SparseCore 0:
  11.1 118.1 all-gather.7
  254.1 60.5 all-gather.11
  316.8 17.9 all-gather.13
  403.1 118.8 all-gather.9
